TPU v7x, 32 devices: a whole 2x2x4 slice. The times are simulated.
32 devices in a mesh: parts: 2 (over y), row: 2 (over core), col: 8 (over z, x).
Axes of the slice: x: 2, y: 2, z: 4, core: 2. Of those that a mesh axis runs over, the one named last changes fastest.
Arguments:
- hidden: bfloat16 [2048, 8192], P(('parts', 'row'), 'col'), parts along dimension 0, may hold values from -6 to 6
- target: bfloat16 [2048, 1024], P(('parts', 'col'), 'row'), parts along dimension 0, may hold values from -6 to 6
- v_weight: bfloat16 [16384, 1024], P(('parts', 'col'), 'row'), parts along dimension 0, may hold values from -0.0625 to 0.0625
- codes: int32 [16384, 1024], P(('parts', 'col'), 'row'), parts along dimension 0, may hold values from -8 to 7
- exponents: int32 [2048], P(('parts', 'row')), parts along dimension 0, may hold values from 7 to 10
- rotation: float32 [8192, 8192], P('col', 'row'), may hold values from -0.0625 to 0.0625
- head_rotation: float32 [256, 128], P('parts'), parts along dimension 0, may hold values from -0.5 to 0.5
Outputs:
- rotation_grad: float32 [16384, 8192], P(('parts', 'col'), 'row'), parts along dimension 0
- head_rotation_grad: float32 [256, 128], P('parts'), parts along dimension 0
There are 2 independent parts, one for each index of `parts`. A program takes and returns all parts, laid end to end along the dimension named above; an argument that names none is the same for every part. Nothing has to cross between parts.
All inputs are finite; a program needn't handle non-finite values.
Results may differ from a plain program's by a relative error of at most 0.0059.
Values may be sent and summed in bfloat16 or wider, within the bound.
A program may use at most 192 MiB of HBM per device.

v0:
```python
import math

import jax
import jax.numpy as jnp
from jax import lax
from jax.sharding import PartitionSpec as P

DH = 128


def on_device(hidden, target, v_weight, codes, exponents, rotation, head_rotation):
    scales = jnp.exp2(-exponents.astype(jnp.float32))
    quantized = (codes.astype(jnp.float32) * scales[None, :]).astype(jnp.bfloat16)
    all_tokens = lax.all_gather(hidden, "row", axis=0, tiled=True)
    token_count = all_tokens.shape[0]
    block = all_tokens
    outputs = lax.psum_scatter(
        jnp.dot(block, quantized, preferred_element_type=jnp.float32),
        "col",
        scatter_dimension=0,
        tiled=True,
    )
    resid = ((outputs - target.astype(jnp.float32)) * (1.0 / math.sqrt(token_count))).astype(
        jnp.bfloat16
    )
    block = all_tokens
    weight_grad = lax.dot_general(
        block,
        lax.all_gather(resid, "col", axis=0, tiled=True),
        (((0,), (0,)), ((), ())),
        preferred_element_type=jnp.float32,
    )
    keep = jnp.where((codes > -8) & (codes < 7), 1.0, 0.0).astype(jnp.float32)
    grad_rot = (keep * weight_grad).astype(jnp.bfloat16)
    head_half = head_rotation.astype(jnp.bfloat16)
    rotated_w = jnp.dot(v_weight.reshape(-1, DH), head_half, preferred_element_type=jnp.float32)
    rotated_w = rotated_w.reshape(v_weight.shape).astype(jnp.bfloat16)
    rotation_rows = lax.all_gather(rotation.astype(jnp.bfloat16), "row", axis=1, tiled=True)
    grad_stripe = lax.all_gather(grad_rot, "col", axis=0, tiled=True)
    carried = jnp.dot(rotation_rows, grad_stripe, preferred_element_type=jnp.float32).astype(
        jnp.bfloat16
    )
    partial_grad = lax.dot_general(
        rotated_w, grad_stripe, (((1,), (1,)), ((), ())), preferred_element_type=jnp.float32
    )
    head_term = lax.dot_general(
        v_weight.reshape(-1, DH),
        carried.reshape(-1, DH),
        (((0,), (0,)), ((), ())),
        preferred_element_type=jnp.float32,
    )
    head_rotation_grad = lax.psum(head_term, ("row", "col"))
    rotation_grad = lax.psum_scatter(partial_grad, "row", scatter_dimension=1, tiled=True)
    return (rotation_grad, head_rotation_grad)


def solution(mesh):
    in_specs = (
        P(("parts", "row"), "col"),
        P(("parts", "col"), "row"),
        P(("parts", "col"), "row"),
        P(("parts", "col"), "row"),
        P(("parts", "row")),
        P("col", "row"),
        P("parts", None),
    )
    out_specs = (P(("parts", "col"), "row"), P("parts", None))
    return jax.shard_map(
        on_device, mesh=mesh, in_specs=in_specs, out_specs=out_specs, check_vma=False
    )
```

profile of v0, /device:TPU:0, one launch (start us, length us, event | category | flops | bytes accessed | tf_op | source)
XLA Modules:
  0.0 453.6 jit_solution(3258741127459313891)
XLA Ops:
  7.2 0.7 all-gather.5.cloned.1.call-update
  7.9 0.7 multiply_exponential_fusion
  8.6 14.2 %all-gather.5.cloned.1.call-done = bf16[1024,1024]{1,0:T(8,128)(2,1)} async-done(((bf16[512,1024]{1,0:T(8,128)(2,1)}), bf16[1024,1024]{1,0:T(8,128)(2,1)}) %all-gather.5.cloned.1.call-update) | async-done | bytes 2097168 | tf_op jit(solution)/shard_map/all_gather | solution.py:14
  22.9 4.8 %convolution_bitcast_fusion = f32[1024,512]{1,0:T(8,128)} fusion(bf16[1024,1024]{1,0:T(8,128)(2,1)} %all-gather.5.cloned.1.call-done, s32[1024,512]{1,0:T(8,128)} %param.10, f32[512]{0:T(512)S(1)} %multiply_exponential_fusion), kind=kOutput, calls=%fused_computation.4 | convolution fusion | flops 1075314688 | bytes 6293504 | tf_op jit(solution)/shard_map/dot_general | solution.py:18
  27.7 68.9 %reduce-scatter.3.cloned.1.call-done = f32[128,512]{1,0:T(8,128)} async-done(((f32[1024,512]{1,0:T(8,128)}), f32[128,512]{1,0:T(8,128)}) %reduce-scatter.3.cloned.1.call-update) | async-done | bytes 262160 | tf_op jit(solution)/shard_map/reduce_scatter | solution.py:17
  96.6 1.7 multiply_convert_fusion.2
  98.3 9.1 %convert_element_type.45 = bf16[1024,4096]{1,0:T(8,128)(2,1)} convert(f32[1024,4096]{1,0:T(8,128)} %param.12) | non-fusion elementwise | flops 4194304 | bytes 25165824 | tf_op jit(solution)/shard_map/convert_element_type | solution.py:38
  107.5 1.5 copy-done
  109.0 1.8 copy.12
  110.8 27.1 %all-gather.7.cloned.1.call-done = bf16[1024,512]{1,0:T(8,128)(2,1)} async-done(((bf16[128,512]{1,0:T(8,128)(2,1)}), bf16[1024,512]{1,0:T(8,128)(2,1)}) %all-gather.7.cloned.1.call-update) | async-done | bytes 1048592 | tf_op jit(solution)/shard_map/all_gather | solution.py:29
  138.0 4.9 %fusion = bf16[1024,512]{0,1:T(8,128)(2,1)} fusion(s32[1024,512]{0,1:T(8,128)} %copy.12, bf16[1024,512]{1,0:T(8,128)(2,1)} %all-gather.7.cloned.1.call-done, bf16[1024,1024]{1,0:T(8,128)(2,1)} %all-gather.5.cloned.1.call-done), kind=kOutput, calls=%fused_computation.2 | convolution fusion | flops 1076887552 | bytes 6291456 | tf_op jit(solution)/shard_map/dot_general | solution.py:27
  142.9 0.7 reshape.14
  143.7 0.4 convolution_convert_fusion
  144.1 1.5 convert_element_type.38
  145.5 23.3 %all-gather.11.cloned.1.call-done = bf16[1024,8192]{1,0:T(8,128)(2,1)} async-done(((bf16[1024,4096]{1,0:T(8,128)(2,1)}), bf16[1024,8192]{1,0:T(8,128)(2,1)}) %all-gather.11.cloned.1.call-update) | async-done | bytes 16777232 | tf_op jit(solution)/shard_map/all_gather | solution.py:38
  168.8 128.1 %all-gather.9.cloned.1.call-done = bf16[8192,512]{0,1:T(8,128)(2,1)} async-done(((bf16[1024,512]{0,1:T(8,128)(2,1)}), bf16[8192,512]{0,1:T(8,128)(2,1)}) %all-gather.9.cloned.1.call-update) | async-done | bytes 8388624 | tf_op jit(solution)/shard_map/all_gather | solution.py:39
  297.0 14.8 %fusion.1 = bf16[1024,512]{0,1:T(8,128)(2,1)S(1)} fusion(bf16[8192,512]{0,1:T(8,128)(2,1)} %all-gather.9.cloned.1.call-done, bf16[1024,8192]{1,0:T(8,128)(2,1)} %all-gather.11.cloned.1.call-done), kind=kOutput, calls=%fused_computation.6 | convolution fusion | flops 8590458880 | bytes 26214400 | tf_op jit(solution)/shard_map/dot_general | solution.py:40
  311.8 0.5 copy.14
  312.4 0.7 reshape.15
  313.0 1.1 convolution_bitcast_fusion.1
  314.3 17.9 %fusion.4 = f32[1024,8192]{1,0:T(8,128)} fusion(bf16[1024,512]{1,0:T(8,128)(2,1)S(1)} %copy-done.2, bf16[8192,512]{0,1:T(8,128)(2,1)} %all-gather.9.cloned.1.call-done), kind=kOutput, calls=%fused_computation.12 | convolution fusion | flops 8589934592 | bytes 42991616 | tf_op jit(solution)/shard_map/dot_general | solution.py:43
  332.2 64.8 %all-reduce.2.cloned.1.call-done = f32[128,128]{0,1:T(8,128)} async-done(((f32[128,128]{0,1:T(8,128)}), f32[128,128]{0,1:T(8,128)}) %all-reduce.2.cloned.1.call-update) | async-done | bytes 65552 | tf_op jit(solution)/shard_map/psum | solution.py:52
  397.0 1.6 copy.15
  398.6 48.2 %reduce-scatter.5.cloned.1.call-done = f32[1024,4096]{1,0:T(8,128)} async-done(((f32[1024,8192]{1,0:T(8,128)}), f32[1024,4096]{1,0:T(8,128)}) %reduce-scatter.5.cloned.1.call-update) | async-done | bytes 16777232 | tf_op jit(solution)/shard_map/reduce_scatter | solution.py:53
  (22 shorter events, 0.5 us)
Async XLA Ops:
  7.2 15.7 %all-gather.5.cloned.1.call-start = ((), (), s32[]{:S(2)}) async-start(), calls=%async_computation.2 | async-start | bytes 3145728 | tf_op jit(solution)/shard_map/all_gather | solution.py:14
  7.9 88.7 %reduce-scatter.3.cloned.1.call-start = ((), (), s32[]{:S(2)}) async-start(), calls=%async_computation.3 | async-start | bytes 2359296 | tf_op jit(solution)/shard_map/reduce_scatter | solution.py:17
  27.7 69.0 %copy-start.3 = (bf16[128,512]{1,0:T(8,128)(2,1)S(1)}, bf16[128,512]{1,0:T(8,128)(2,1)}, u32[]{:S(2)}) copy-start(bf16[128,512]{1,0:T(8,128)(2,1)} %param.8) | copy-start | bytes 393220
  27.7 110.3 %all-gather.7.cloned.1.call-start = ((), (), s32[]{:S(2)}) async-start(), calls=%async_computation.4 | async-start | bytes 1179648 | tf_op jit(solution)/shard_map/all_gather | solution.py:29
  98.3 70.5 %all-gather.11.cloned.1.call-start = ((), (), s32[]{:S(2)}) async-start(), calls=%async_computation.7 | async-start | bytes 25165824 | tf_op jit(solution)/shard_map/all_gather | solution.py:38
  107.4 1.6 copy-start
  107.4 189.5 %all-gather.9.cloned.1.call-start = ((), (), s32[]{:S(2)}) async-start(), calls=%async_computation.5 | async-start | bytes 9437184 | tf_op jit(solution)/shard_map/all_gather | solution.py:39
  110.8 32.1 %copy-start.1 = (bf16[1024,512]{1,0:T(8,128)(2,1)S(1)}, bf16[1024,512]{1,0:T(8,128)(2,1)}, u32[]{:S(2)}) copy-start(bf16[1024,512]{1,0:T(8,128)(2,1)} %param.9) | copy-start | bytes 3145732
  142.8 0.8 copy-start.4
  142.8 254.2 %all-reduce.2.cloned.1.call-start = ((), (), s32[]{:S(2)}) async-start(), calls=%async_computation.8 | async-start | bytes 131072 | tf_op jit(solution)/shard_map/psum | solution.py:52
  313.0 1.2 copy-start.2
  314.2 132.6 %reduce-scatter.5.cloned.1.call-start = ((), (), s32[]{:S(2)}) async-start(), calls=%async_computation.6 | async-start | bytes 50331648 | tf_op jit(solution)/shard_map/reduce_scatter | solution.py:53
Sparse Core Ops, SparseCore 0:
  9.5 13.2 all-gather.4
  27.8 68.7 reduce-scatter.2
  98.8 39.1 all-gather.6
  139.9 28.8 all-gather.10
  170.8 126.0 all-gather.8
  314.3 82.6 all-reduce.1
  400.0 46.7 reduce-scatter.4
where the time goes:
time: 454 us
  waiting for transfers between devices  375 us (83%)
  matrix products  43.9 us (10%)
  between operations  14.2 us (3%)
  other arithmetic  11.4 us (3%)
  local copies, waits for them, and re-layouts  8.4 us (2%)
    all_gather x1, waiting for transfers between devices, on_device(): grad_stripe = lax.all_gather(grad_rot, 'col', axis=0, tiled=True)  128 us
    reduce_scatter x1, waiting for transfers between devices, on_device(): lax.psum_scatter(jnp.dot(block, quantized, preferred_element_type=jnp.flo...  68.9 us
    psum x1, waiting for transfers between devices, on_device(): head_rotation_grad = lax.psum(head_term, ('row', 'col'))  64.8 us
    reduce_scatter x1, waiting for transfers between devices, on_device(): lax.psum_scatter(partial_grad, 'row', scatter_dimension=1, tiled=True)  48.2 us
    all_gather x1, waiting for transfers between devices, on_device(): lax.all_gather(resid, 'col', axis=0, tiled=True)  27.1 us
    all_gather x1, waiting for transfers between devices, on_device(): lax.all_gather(rotation.astype(jnp.bfloat16), 'row', axis=1, tiled=True)  23.3 us
    dot_general x1, matrix products, on_device(): lax.dot_general(rotated_w, grad_stripe, (((1,), (1,)), ((), ())), preferr...  17.9 us
    dot_general x1, matrix products, on_device(): jnp.dot(rotation_rows, grad_stripe, preferred_element_type=jnp.float32)  14.8 us
  transfers between devices with their start and end apart: 7, of which 7 were waited for; matrix products, arithmetic and copies ran while one was open for 8% of the time, Pallas kernels for 0%

commit v1 on v0

v1 whole, which is shorter than its diff:
```python
import math

import jax
import jax.numpy as jnp
from jax import lax
from jax.sharding import PartitionSpec as P

DH = 128


def on_device(hidden, target, v_weight, codes, exponents, rotation, head_rotation):
    cols = lax.axis_size("col")
    scales = jnp.exp2(-exponents.astype(jnp.float32))
    quantized = (codes.astype(jnp.float32) * scales[None, :]).astype(jnp.bfloat16)
    all_tokens = lax.all_gather(hidden, "row", axis=0, tiled=True)
    v_full = lax.all_gather(v_weight, "row", axis=1, tiled=True)
    token_count = all_tokens.shape[0]
    partial = jnp.dot(all_tokens, quantized, preferred_element_type=jnp.float32)
    pieces = partial.astype(jnp.bfloat16).reshape(cols, token_count // cols, -1)
    pieces = lax.all_to_all(pieces, "col", split_axis=0, concat_axis=0, tiled=True)
    outputs = jnp.sum(pieces.astype(jnp.float32), axis=0)
    resid = ((outputs - target.astype(jnp.float32)) * (1.0 / math.sqrt(token_count))).astype(
        jnp.bfloat16
    )
    weight_grad = lax.dot_general(
        all_tokens,
        lax.all_gather(resid, "col", axis=0, tiled=True),
        (((0,), (0,)), ((), ())),
        preferred_element_type=jnp.float32,
    )
    keep = jnp.where((codes > -8) & (codes < 7), 1.0, 0.0).astype(jnp.float32)
    grad_rot = (keep * weight_grad).astype(jnp.bfloat16)
    head_half = head_rotation.astype(jnp.bfloat16)
    rotated_w = jnp.dot(v_full.reshape(-1, DH), head_half, preferred_element_type=jnp.float32)
    rotated_w = rotated_w.reshape(v_full.shape).astype(jnp.bfloat16)
    stripe = lax.all_gather(grad_rot, "col", axis=0, tiled=True)
    stripe = lax.all_to_all(stripe, "row", split_axis=0, concat_axis=1, tiled=True)
    rotation_grad = lax.dot_general(
        rotated_w, stripe, (((1,), (1,)), ((), ())), preferred_element_type=jnp.float32
    )
    carried = jnp.dot(
        rotation.astype(jnp.bfloat16), stripe, preferred_element_type=jnp.float32
    ).astype(jnp.bfloat16)
    head_term = lax.dot_general(
        v_full.reshape(-1, DH),
        carried.reshape(-1, DH),
        (((0,), (0,)), ((), ())),
        preferred_element_type=jnp.float32,
    )
    head_rotation_grad = lax.psum(head_term, ("row", "col"))
    return (rotation_grad, head_rotation_grad)


def solution(mesh):
    in_specs = (
        P(("parts", "row"), "col"),
        P(("parts", "col"), "row"),
        P(("parts", "col"), "row"),
        P(("parts", "col"), "row"),
        P(("parts", "row")),
        P("col", "row"),
        P("parts", None),
    )
    out_specs = (P(("parts", "col"), "row"), P("parts", None))
    return jax.shard_map(
        on_device, mesh=mesh, in_specs=in_specs, out_specs=out_specs, check_vma=False
    )
```

time: 454 us -> 379 us (0.83)
  waiting for transfers between devices: 375 us -> 270 us
  local copies, waits for them, and re-layouts: 8.4 us -> 30.9 us
  blocking collectives: 0 us -> 12.1 us
  other arithmetic: 11.4 us -> 1.53 us
  starting transfers between devices: 0.28 us -> 5.97 us
    reduce_scatter x2 -> x0, waiting for transfers between devices: 117 us -> none  [the longest x1 68.9 us: on_device(): lax.psum_scatter(jnp.dot(block, quantized, preferred_element_type=jnp.flo...]
    all_gather x2, waiting for transfers between devices: 151 us -> 125 us  [the longest x1 119 us: on_device(): stripe = lax.all_gather(grad_rot, 'col', axis=0, tiled=True)]
    all_to_all x0 -> x1, waiting for transfers between devices: none -> 26 us  [on_device(): lax.all_to_all(pieces, 'col', split_axis=0, concat_axis=0, tiled=True)]
    all_to_all x0 -> x1, blocking collectives: none -> 12.1 us  [on_device(): lax.all_to_all(stripe, 'row', split_axis=0, concat_axis=1, tiled=True)]
    convert_element_type x1 -> x0, other arithmetic: 9.06 us -> none  [on_device(): rotation.astype(jnp.bfloat16)]
    all_gather x1, waiting for transfers between devices: 27.1 us -> 36.1 us  [on_device(): lax.all_gather(resid, 'col', axis=0, tiled=True)]
    all_to_all x0 -> x1, local copies, waits for them, and re-layouts: none -> 7.89 us  [on_device(): lax.all_to_all(stripe, 'row', split_axis=0, concat_axis=1, tiled=True)]
    convert_element_type x2, local copies, waits for them, and re-layouts: 2.01 us -> 8.14 us  [the longest x1 4.21 us: on_device(): rotated_w = rotated_w.reshape(v_full.shape).astype(jnp.bfloat16)]
  transfers between devices with their start and end apart: 7 -> 6, of which waited for: 7 -> 6; matrix products, arithmetic and copies ran while one was open for 8% -> 9% of each run, Pallas kernels for 0% -> 0%
where the time goes in v1:
time: 379 us; the launch traced here: 377 us
  waiting for transfers between devices  270 us (71%)
  matrix products  43 us (11%)
  local copies, waits for them, and re-layouts  30.9 us (8%)
  between operations  13.8 us (4%)
  blocking collectives  12.1 us (3%)
  starting transfers between devices  5.97 us (2%)
    all_gather x1, waiting for transfers between devices, on_device(): stripe = lax.all_gather(grad_rot, 'col', axis=0, tiled=True)  119 us
    psum x1, waiting for transfers between devices, on_device(): head_rotation_grad = lax.psum(head_term, ('row', 'col'))  66.6 us
    all_gather x1, waiting for transfers between devices, on_device(): lax.all_gather(resid, 'col', axis=0, tiled=True)  36.1 us
    all_to_all x1, waiting for transfers between devices, on_device(): lax.all_to_all(pieces, 'col', split_axis=0, concat_axis=0, tiled=True)  26 us
    dot_general x1, matrix products, on_device(): lax.dot_general(rotated_w, stripe, (((1,), (1,)), ((), ())), preferred_el...  16.2 us
    all_gather x1, waiting for transfers between devices, on_device(): all_tokens = lax.all_gather(hidden, 'row', axis=0, tiled=True)  14.3 us
    dot_general x1, matrix products, on_device(): jnp.dot(rotation.astype(jnp.bfloat16), stripe, preferred_element_type=jnp...  13.5 us
    all_to_all x1, blocking collectives, on_device(): lax.all_to_all(stripe, 'row', split_axis=0, concat_axis=1, tiled=True)  12.1 us
  transfers between devices with their start and end apart: 6, of which 6 were waited for; matrix products, arithmetic and copies ran while one was open for 9% of the time, Pallas kernels for 0%

profile of v1, /device:TPU:0, one launch (start us, length us, event | category | flops | bytes accessed | tf_op | source)
XLA Modules:
  0.0 377.1 jit_solution(3277294903130088989)
XLA Ops:
  8.6 14.3 %all-gather.7.cloned.1.call-done = bf16[1024,1024]{1,0:T(8,128)(2,1)} async-done(((bf16[512,1024]{1,0:T(8,128)(2,1)}), bf16[1024,1024]{1,0:T(8,128)(2,1)}) %all-gather.7.cloned.1.call-update) | async-done | bytes 2097168 | tf_op jit(solution)/shard_map/all_gather | solution.py:15
  22.9 3.5 fusion.5
  26.4 1.2 copy.31
  27.6 5.8 %all-to-all-start = ((bf16[8,128,512]{1,2,0:T(8,128)(2,1)}), bf16[8,128,512]{1,2,0:T(8,128)(2,1)S(1)}, u32[]{:S(2)}, u32[]{:S(2)}) async-start(bf16[8,128,512]{1,2,0:T(8,128)(2,1)} %bitcast.29), calls=%async_computation | async-start | bytes 2097152 | tf_op jit(solution)/shard_map/all_to_all | solution.py:20
  33.5 26.0 %all-to-all-done = bf16[8,128,512]{1,2,0:T(8,128)(2,1)S(1)} async-done(((bf16[8,128,512]{1,2,0:T(8,128)(2,1)}), bf16[8,128,512]{1,2,0:T(8,128)(2,1)S(1)}, u32[]{:S(2)}, u32[]{:S(2)}) %all-to-all-start) | async-done | bytes 1048608 | tf_op jit(solution)/shard_map/all_to_all | solution.py:20
  59.7 0.7 multiply_convert_fusion.2
  61.2 1.8 copy.17
  63.0 36.1 %all-gather.9.cloned.1.call-done = bf16[1024,512]{0,1:T(8,128)(2,1)} async-done(((bf16[128,512]{0,1:T(8,128)(2,1)}), bf16[1024,512]{0,1:T(8,128)(2,1)}) %all-gather.9.cloned.1.call-update) | async-done | bytes 1048592 | tf_op jit(solution)/shard_map/all_gather | solution.py:27
  99.2 4.8 %fusion.2 = bf16[1024,512]{0,1:T(8,128)(2,1)} fusion(s32[1024,512]{0,1:T(8,128)} %copy.17, bf16[1024,512]{0,1:T(8,128)(2,1)} %all-gather.9.cloned.1.call-done, bf16[1024,1024]{1,0:T(8,128)(2,1)} %all-gather.7.cloned.1.call-done), kind=kOutput, calls=%fused_computation.5 | convolution fusion | flops 1076887552 | bytes 6291456 | tf_op jit(solution)/shard_map/dot_general | solution.py:25
  104.0 6.2 %all-gather.5.cloned.1.call-done = bf16[1024,1024]{1,0:T(8,128)(2,1)} async-done(((bf16[1024,512]{1,0:T(8,128)(2,1)}), bf16[1024,1024]{1,0:T(8,128)(2,1)}) %all-gather.5.cloned.1.call-update) | async-done | bytes 2097168 | tf_op jit(solution)/shard_map/all_gather | solution.py:16
  110.2 2.8 reshape.20
  113.0 2.0 convolution_convert_fusion
  115.1 4.2 %convert_element_type.47 = bf16[1024,1024]{1,0:T(8,128)(2,1)} reshape(bf16[8192,128]{1,0:T(8,128)(2,1)} %convolution_convert_fusion) | data formatting | bytes 4194304 | tf_op jit(solution)/shard_map/convert_element_type | solution.py:35
  119.3 119.1 %all-gather.11.cloned.1.call-done = bf16[8192,512]{0,1:T(8,128)(2,1)} async-done(((bf16[1024,512]{0,1:T(8,128)(2,1)}), bf16[8192,512]{0,1:T(8,128)(2,1)}) %all-gather.11.cloned.1.call-update) | async-done | bytes 8388624 | tf_op jit(solution)/shard_map/all_gather | solution.py:36
  238.4 7.9 %copy.30 = bf16[64,2,8,4096]{3,2,0,1:T(8,128)(2,1)} copy(bf16[64,2,8,4096]{3,2,1,0:T(8,128)(2,1)} %bitcast.31) | data formatting | bytes 16777216 | tf_op jit(solution)/shard_map/all_to_all | solution.py:37
  246.2 12.1 %all_to_all.24 = bf16[2,4096,512]{1,2,0:T(8,128)(2,1)S(1)} all-to-all(bf16[2,4096,512]{1,2,0:T(8,128)(2,1)} %bitcast.30), channel_id=1, replica_groups=mesh['parts'=2,'row'=2,'col'=8] {'row'}, dimensions={0} | all-to-all | bytes 16777216 | tf_op jit(solution)/shard_map/all_to_all | solution.py:37
  258.3 3.2 copy-done
  261.5 13.5 %convert_bitcast_fusion = bf16[1024,1024]{0,1:T(8,128)(2,1)} fusion(bf16[4096,1024]{0,1:T(8,128)(2,1)S(1)} %bitcast.32, f32[1024,4096]{1,0:T(8,128)} %param.12), kind=kOutput, calls=%fused_computation.6 | convolution fusion | flops 8595177472 | bytes 27262976 | tf_op jit(solution)/shard_map/dot_general | solution.py:41
  275.1 3.9 %copy.23 = bf16[1024,1024]{1,0:T(8,128)(2,1)} copy(bf16[1024,1024]{0,1:T(8,128)(2,1)} %convert_bitcast_fusion) | data formatting | bytes 4194304 | tf_op jit(solution)/shard_map/convert_element_type | solution.py:43
  279.0 4.2 %reshape.22 = bf16[8192,128]{1,0:T(8,128)(2,1)} reshape(bf16[1024,1024]{1,0:T(8,128)(2,1)} %copy.23) | data formatting | bytes 4194304 | tf_op jit(solution)/shard_map/reshape | solution.py:46
  283.2 3.0 convolution_bitcast_fusion
  286.2 16.2 %fusion.8 = f32[1024,4096]{1,0:T(8,128)} fusion(bf16[1024,1024]{1,0:T(8,128)(2,1)} %convert_element_type.47, bf16[4096,1024]{0,1:T(8,128)(2,1)} %bitcast.33), kind=kOutput, calls=%fused_computation.17 | convolution fusion | flops 8589934592 | bytes 27262976 | tf_op jit(solution)/shard_map/dot_general | solution.py:38
  302.3 66.6 %all-reduce.2.cloned.1.call-done = f32[128,128]{0,1:T(8,128)} async-done(((f32[128,128]{0,1:T(8,128)}), f32[128,128]{0,1:T(8,128)}) %all-reduce.2.cloned.1.call-update) | async-done | bytes 65552 | tf_op jit(solution)/shard_map/psum | solution.py:50
  369.0 1.6 copy.24
  (20 shorter events, 2.6 us)
Async XLA Ops:
  7.2 15.7 %all-gather.7.cloned.1.call-start = ((), (), s32[]{:S(2)}) async-start(), calls=%async_computation.3 | async-start | bytes 3145728 | tf_op jit(solution)/shard_map/all_gather | solution.py:15
  26.4 7.0 %copy-start.2 = (bf16[128,512]{1,0:T(8,128)(2,1)S(1)}, bf16[128,512]{1,0:T(8,128)(2,1)}, u32[]{:S(2)}) copy-start(bf16[128,512]{1,0:T(8,128)(2,1)} %param.8) | copy-start | bytes 393220
  27.6 32.0 %all-to-all-start = ((bf16[8,128,512]{1,2,0:T(8,128)(2,1)}), bf16[8,128,512]{1,2,0:T(8,128)(2,1)S(1)}, u32[]{:S(2)}, u32[]{:S(2)}) async-start(bf16[8,128,512]{1,2,0:T(8,128)(2,1)} %bitcast.29), calls=%async_computation | async-start | bytes 2097152 | tf_op jit(solution)/shard_map/all_to_all | solution.py:20
  33.3 27.9 %copy-start.1 = (s32[1024,512]{1,0:T(8,128)S(1)}, s32[1024,512]{1,0:T(8,128)}, u32[]{:S(2)}) copy-start(s32[1024,512]{1,0:T(8,128)} %param.10) | copy-start | bytes 6291460
  33.3 65.8 %all-gather.9.cloned.1.call-start = ((), (), s32[]{:S(2)}) async-start(), calls=%async_computation.4 | async-start | bytes 1179648 | tf_op jit(solution)/shard_map/all_gather | solution.py:27
  60.4 49.8 %all-gather.5.cloned.1.call-start = ((), (), s32[]{:S(2)}) async-start(), calls=%async_computation.2 | async-start | bytes 3145728 | tf_op jit(solution)/shard_map/all_gather | solution.py:16
  61.2 177.2 %all-gather.11.cloned.1.call-start = ((), (), s32[]{:S(2)}) async-start(), calls=%async_computation.5 | async-start | bytes 9437184 | tf_op jit(solution)/shard_map/all_gather | solution.py:36
  104.0 9.1 %copy-start.3 = (f32[128,128]{1,0:T(8,128)S(1)}, f32[128,128]{1,0:T(8,128)}, u32[]{:S(2)}) copy-start(f32[128,128]{1,0:T(8,128)} %param.13) | copy-start | bytes 196612
  104.0 265.0 %all-reduce.2.cloned.1.call-start = ((), (), s32[]{:S(2)}) async-start(), calls=%async_computation.6 | async-start | bytes 131072 | tf_op jit(solution)/shard_map/psum | solution.py:50
  258.3 3.2 copy-start
Sparse Core Ops, SparseCore 0:
  9.5 13.2 all-gather.6
  60.5 38.5 all-gather.8
  100.7 9.4 all-gather.4
  112.2 126.0 all-gather.10
  286.3 82.6 all-reduce.1

commit v2 on v1

--- a/solution.py
+++ b/solution.py
@@ -1,11 +1,17 @@
+import functools
 import math
 
 import jax
 import jax.numpy as jnp
 from jax import lax
+from jax.experimental import pallas as pl
+from jax.experimental.pallas import tpu as pltpu
 from jax.sharding import PartitionSpec as P
 
 DH = 128
+MESH = pl.DeviceIdType.MESH
+F32 = jnp.float32
+BF16 = jnp.bfloat16
 
 
 def on_device(hidden, target, v_weight, codes, exponents, rotation, head_rotation):
@@ -51,6 +57,462 @@
     return (rotation_grad, head_rotation_grad)
 
 
+ZS = 4
+
+
+def kernel(
+    token_count,
+    hidden,
+    target,
+    v_weight,
+    codes,
+    scales,
+    head_half,
+    rotation,
+    rot_grad,
+    head_grad,
+    hid,
+    vf,
+    rw,
+    part,
+    part_own,
+    arrived,
+    resid,
+    g_own,
+    g_all,
+    rot32,
+    rot16,
+    carried,
+    stage,
+    head_term,
+    head_in,
+    head_out,
+    swap_send,
+    swap_recv,
+    rs_send,
+    rs_recv,
+    ag_own,
+    ag_z,
+    ag_x,
+    ag_recv,
+    g_src,
+    g_z,
+    g_x,
+    g_recv,
+    rot_sem,
+    out_sem,
+    hs_send,
+    hs_recv,
+    hb_send,
+    hb_recv,
+):
+    r, c = lax.axis_index("row"), lax.axis_index("col")
+    z, x = c // 2, c % 2
+    me = c * 2 + r
+    cols, people = 2 * ZS, 4 * ZS
+    width, chans = codes.shape
+    half_tokens = hidden.shape[0]
+    piece = target.shape[0]
+    tile = min(256, chans)
+    wtile = min(256, width)
+
+    def copy(src, dst, send, recv, cc, rr):
+        return pltpu.make_async_remote_copy(
+            src_ref=src,
+            dst_ref=dst,
+            send_sem=send,
+            recv_sem=recv,
+            device_id={"col": cc, "row": rr},
+            device_id_type=MESH,
+        )
+
+    def rot_copy(b):
+        return pltpu.make_async_copy(
+            rotation.at[:, pl.ds(b * width, width)], rot32.at[b % 2], rot_sem.at[b]
+        )
+
+    rot_copy(0).start()
+    rot_copy(1).start()
+
+    barrier = pltpu.get_barrier_semaphore()
+    for d in range(1, people):
+        other = lax.rem(me + d, people)
+        pl.semaphore_signal(
+            barrier, inc=1, device_id={"col": other // 2, "row": other % 2}, device_id_type=MESH
+        )
+    pl.semaphore_wait(barrier, people - 1)
+
+    swap_h = copy(hidden, hid.at[r], swap_send.at[0], swap_recv.at[0], c, 1 - r)
+    swap_v = copy(v_weight, vf.at[r], swap_send.at[1], swap_recv.at[1], c, 1 - r)
+    swap_h.start()
+    swap_v.start()
+    hid[r] = hidden[...]
+    vf[r] = v_weight[...]
+
+    quantized = (codes[...].astype(F32) * scales[...]).astype(BF16)
+
+    def partial_half(h):
+        product = jnp.dot(hid[h], quantized, preferred_element_type=F32)
+        for i in range(ZS):
+            owner = h * ZS + i
+            rows = product[i * piece : (i + 1) * piece]
+            part[owner] = rows.astype(BF16)
+
+            @pl.when(owner == c)
+            def _():
+                part_own[...] = rows
+
+        def send(i, carry):
+            owner = h * ZS + lax.rem(c + i, ZS)
+
+            @pl.when(owner != c)
+            def _():
+                copy(
+                    part.at[owner], arrived.at[c], rs_send.at[owner], rs_recv.at[c], owner, r
+                ).start()
+
+            return carry
+
+        lax.fori_loop(0, ZS, send, 0)
+
+    partial_half(r)
+    swap_h.wait_recv()
+    partial_half(1 - r)
+
+    def round_rotation(b):
+        rot_copy(b).wait()
+
+        def body(i, carry):
+            rows = pl.ds(pl.multiple_of(i * 128, 128), 128)
+            rot16[b, rows, :] = rot32[b % 2, rows, :].astype(BF16)
+            return carry
+
+        lax.fori_loop(0, width // 128, body, 0)
+        if b + 2 < ZS:
+            rot_copy(b + 2).start()
+
+    round_rotation(0)
+    round_rotation(1)
+    swap_v.wait_recv()
+    for k in range(2):
+        for n in range(chans // DH):
+            cut = slice(n * DH, (n + 1) * DH)
+            rw[k, :, cut] = jnp.dot(
+                vf[k, :, cut], head_half[...], preferred_element_type=F32
+            ).astype(BF16)
+
+    total = part_own[...] - target[...].astype(F32)
+    for d in range(1, cols):
+        s = lax.rem(c + d, cols)
+        copy(part.at[s], arrived.at[s], rs_send.at[s], rs_recv.at[s], s, r).wait_recv()
+        total = total + arrived[s].astype(F32)
+    resid[c] = (total * (1.0 / math.sqrt(token_count))).astype(BF16)
+
+    def ag_copy(s, sem, cc):
+        return copy(resid.at[s], resid.at[s], sem, ag_recv.at[s], cc, r)
+
+    def ag_first(act):
+        @pl.when(z < ZS - 1)
+        def _():
+            act(ag_copy(c, ag_own.at[0], c + 2))
+
+        @pl.when(z > 0)
+        def _():
+            act(ag_copy(c, ag_own.at[1], c - 2))
+
+        act(ag_copy(c, ag_own.at[2], 2 * z + 1 - x))
+
+    def ag_next(s, up, act):
+        if up:
+
+            @pl.when(z < ZS - 1)
+            def _():
+                act(ag_copy(s, ag_z.at[s], c + 2))
+
+        else:
+
+            @pl.when(z > 0)
+            def _():
+                act(ag_copy(s, ag_z.at[s], c - 2))
+
+        act(ag_copy(s, ag_x.at[s], 2 * z + 1 - x))
+
+    start = lambda cp: cp.start()
+    sent = lambda cp: cp.wait_send()
+
+    ag_first(start)
+    round_rotation(2)
+    for d in range(1, ZS):
+
+        @pl.when(z >= d)
+        def _():
+            s = c - 2 * d
+            ag_copy(s, ag_z.at[s], c).wait_recv()
+            ag_next(s, True, start)
+
+        @pl.when(z + d < ZS)
+        def _():
+            s = c + 2 * d
+            ag_copy(s, ag_z.at[s], c).wait_recv()
+            ag_next(s, False, start)
+
+    round_rotation(3)
+    for zz in range(ZS):
+        s = 2 * zz + 1 - x
+        ag_copy(s, ag_z.at[s], c).wait_recv()
+
+    home = z // 2
+    for n in range(chans // tile):
+        cut = slice(n * tile, (n + 1) * tile)
+        cot = resid[:, :, cut].reshape(token_count, tile)
+        grad = lax.dot_general(
+            hid[...].reshape(token_count, width),
+            cot,
+            (((0,), (0,)), ((), ())),
+            preferred_element_type=F32,
+        )
+        kept = (codes[:, cut] > -8) & (codes[:, cut] < 7)
+        g_own[:, cut] = jnp.where(kept, grad, 0.0).astype(BF16)
+
+    def g_copy(src, slot, k, sem, cc, core):
+        return copy(src, g_all.at[slot, k], sem, g_recv.at[slot * 2 + k], cc, core)
+
+    mine = lax.rem(c, ZS)
+
+    def g_first(act):
+        @pl.when(z < ZS - 1)
+        def _():
+            act(g_copy(g_own, mine, r, g_src.at[0], c + 2, home))
+
+        @pl.when(z > 0)
+        def _():
+            act(g_copy(g_own, mine, r, g_src.at[1], c - 2, home))
+
+        act(g_copy(g_own, mine, r, g_src.at[2], 2 * z + 1 - x, home))
+
+        @pl.when(r != home)
+        def _():
+            act(g_copy(g_own, mine, r, g_src.at[3], c, home))
+
+    g_first(start)
+
+    @pl.when(r == home)
+    def _():
+        g_all[mine, r] = g_own[...]
+
+    def g_next(zs, k, act):
+        slot = lax.rem(2 * zs + x, ZS)
+        i = slot * 2 + k
+        block = g_all.at[slot, k]
+
+        @pl.when((zs < z) & (z < ZS - 1))
+        def _():
+            act(g_copy(block, slot, k, g_z.at[i], c + 2, r))
+
+        @pl.when((zs > z) & (z > 0))
+        def _():
+            act(g_copy(block, slot, k, g_z.at[i], c - 2, r))
+
+        @pl.when(zs != z)
+        def _():
+            act(g_copy(block, slot, k, g_x.at[i], 2 * z + 1 - x, r))
+
+    near = jnp.clip(z, 2 * r, 2 * r + 1)
+    far = 4 * r + 1 - near
+
+    def out_copy(slot, n):
+        return pltpu.make_async_copy(
+            stage.at[n], rot_grad.at[:, pl.ds(pl.multiple_of(slot * width, 128), width)], out_sem.at[n]
+        )
+
+    def work(slot, n, first):
+        if n >= 2:
+            out_copy(slot, n % 2).wait()
+
+        def outputs(i, carry):
+            rows = pl.ds(pl.multiple_of(i * wtile, wtile), wtile)
+            contract = (((1,), (1,)), ((), ()))
+            stage[n % 2, :, rows] = lax.dot_general(
+                rw[0], g_all[slot, 0, rows, :], contract, preferred_element_type=F32
+            ) + lax.dot_general(
+                rw[1], g_all[slot, 1, rows, :], contract, preferred_element_type=F32
+            )
+            return carry
+
+        lax.fori_loop(0, width // wtile, outputs, 0)
+        out_copy(slot, n % 2).start()
+
+        def carry_on(i, carry):
+            k = i // (chans // tile)
+            cut = pl.ds(pl.multiple_of(lax.rem(i, chans // tile) * tile, tile), tile)
+            product = jnp.dot(rot16[slot], g_all[slot, k, :, cut], preferred_element_type=F32)
+            if first:
+                carried[k, :, cut] = product
+            else:
+                carried[k, :, cut] += product
+            return carry
+
+        lax.fori_loop(0, 2 * (chans // tile), carry_on, 0)
+
+    def g_wait(slot, k):
+        copy(g_own, g_all.at[slot, k], g_src.at[0], g_recv.at[slot * 2 + k], c, r).wait_recv()
+
+    n = 0
+    for zs in (near, far):
+        slot = lax.rem(2 * zs + x, ZS)
+        for k in range(2):
+
+            @pl.when((zs != z) | (r != k))
+            def _():
+                g_wait(slot, k)
+
+            g_next(zs, k, start)
+        work(slot, n, n == 0)
+        n += 1
+    for zs in (near, far):
+        slot = lax.rem(2 * zs + 1 - x, ZS)
+        for k in range(2):
+            g_wait(slot, k)
+        work(slot, n, False)
+        n += 1
+
+    term = jnp.zeros((DH, DH), F32)
+    for k in range(2):
+        for n in range(chans // DH):
+            cut = slice(n * DH, (n + 1) * DH)
+            term = term + lax.dot_general(
+                vf[k, :, cut],
+                carried[k, :, cut].astype(BF16),
+                (((0,), (0,)), ((), ())),
+                preferred_element_type=F32,
+            )
+    share = DH // people
+    head_term[...] = term.reshape(people, share, DH)
+
+    def hs_copy(d):
+        other = lax.rem(me + d, people)
+        return copy(
+            head_term.at[other],
+            head_in.at[me],
+            hs_send.at[other],
+            hs_recv.at[me],
+            other // 2,
+            other % 2,
+        )
+
+    def hb_copy(d):
+        other = lax.rem(me + d, people)
+        return copy(
+            head_out.at[me],
+            head_out.at[me],
+            hb_send.at[other],
+            hb_recv.at[me],
+            other // 2,
+            other % 2,
+        )
+
+    for d in range(1, people):
+        hs_copy(d).start()
+    total = head_term[me]
+    for d in range(1, people):
+        s = lax.rem(me + d, people)
+        copy(head_in.at[s], head_in.at[s], hs_send.at[s], hs_recv.at[s], c, r).wait_recv()
+        total = total + head_in[s]
+    head_out[me] = total
+    for d in range(1, people):
+        hb_copy(d).start()
+    for d in range(1, people):
+        s = lax.rem(me + d, people)
+        copy(head_out.at[s], head_out.at[s], hb_send.at[s], hb_recv.at[s], c, r).wait_recv()
+    head_grad[...] = head_out[...].reshape(DH, DH)
+
+    for d in range(1, people):
+        hs_copy(d).wait_send()
+        hb_copy(d).wait_send()
+    swap_h.wait_send()
+    swap_v.wait_send()
+    for d in range(1, cols):
+        s = lax.rem(c + d, cols)
+        copy(part.at[s], arrived.at[c], rs_send.at[s], rs_recv.at[c], s, r).wait_send()
+    ag_first(sent)
+    for d in range(1, ZS):
+
+        @pl.when(z >= d)
+        def _():
+            ag_next(c - 2 * d, True, sent)
+
+        @pl.when(z + d < ZS)
+        def _():
+            ag_next(c + 2 * d, False, sent)
+
+    g_first(sent)
+    for zs in (near, far):
+        for k in range(2):
+            g_next(zs, k, sent)
+    out_copy(0, 0).wait()
+    out_copy(0, 1).wait()
+
+
+def on_grid(hidden, target, v_weight, codes, exponents, rotation, head_rotation):
+    width, chans = codes.shape
+    piece = target.shape[0]
+    cols, people = 2 * ZS, 4 * ZS
+    token_count = 2 * hidden.shape[0]
+    scales = jnp.exp2(-exponents.astype(F32))[None, :]
+    head_half = head_rotation.astype(BF16)
+    vmem = pl.BlockSpec(memory_space=pltpu.VMEM)
+    anywhere = pl.BlockSpec(memory_space=pl.ANY)
+    dma = pltpu.SemaphoreType.DMA
+    return pl.pallas_call(
+        functools.partial(kernel, token_count),
+        out_shape=(
+            jax.ShapeDtypeStruct(rotation.shape, F32),
+            jax.ShapeDtypeStruct((DH, DH), F32),
+        ),
+        in_specs=[vmem] * 6 + [anywhere],
+        out_specs=(anywhere, vmem),
+        scratch_shapes=[
+            pltpu.VMEM((2,) + hidden.shape, BF16),
+            pltpu.VMEM((2, width, chans), BF16),
+            pltpu.VMEM((2, width, chans), BF16),
+            pltpu.VMEM((cols, piece, chans), BF16),
+            pltpu.VMEM((piece, chans), F32),
+            pltpu.VMEM((cols, piece, chans), BF16),
+            pltpu.VMEM((cols, piece, chans), BF16),
+            pltpu.VMEM((width, chans), BF16),
+            pltpu.VMEM((ZS, 2, width, chans), BF16),
+            pltpu.VMEM((2, width, width), F32),
+            pltpu.VMEM((ZS, width, width), BF16),
+            pltpu.VMEM((2, width, chans), F32),
+            pltpu.VMEM((2, width, width), F32),
+            pltpu.VMEM((people, DH // people, DH), F32),
+            pltpu.VMEM((people, DH // people, DH), F32),
+            pltpu.VMEM((people, DH // people, DH), F32),
+            dma((2,)),
+            dma((2,)),
+            dma((cols,)),
+            dma((cols,)),
+            dma((3,)),
+            dma((cols,)),
+            dma((cols,)),
+            dma((cols,)),
+            dma((4,)),
+            dma((cols,)),
+            dma((cols,)),
+            dma((cols,)),
+            dma((ZS,)),
+            dma((2,)),
+            dma((people,)),
+            dma((people,)),
+            dma((people,)),
+            dma((people,)),
+        ],
+        compiler_params=pltpu.CompilerParams(
+            collective_id=0, has_side_effects=True, vmem_limit_bytes=62 * 1024 * 1024
+        ),
+    )(hidden, target, v_weight, codes, scales, head_half, rotation)
+
+
 def solution(mesh):
     in_specs = (
         P(("parts", "row"), "col"),
@@ -62,6 +524,11 @@
         P("parts", None),
     )
     out_specs = (P(("parts", "col"), "row"), P("parts", None))
+    routed = mesh.shape["col"] == 2 * ZS and mesh.shape["row"] == 2
     return jax.shard_map(
-        on_device, mesh=mesh, in_specs=in_specs, out_specs=out_specs, check_vma=False
+        on_grid if routed else on_device,
+        mesh=mesh,
+        in_specs=in_specs,
+        out_specs=out_specs,
+        check_vma=False,
     )

time: 379 us -> 177 us (0.47)
  waiting for transfers between devices: 270 us -> 0 us
  Pallas kernels: 0 us -> 161 us
  matrix products: 43 us -> 0 us
  local copies, waits for them, and re-layouts: 30.9 us -> 12.4 us
  between operations: 13.8 us -> 0.65 us
  blocking collectives: 12.1 us -> 0 us
  starting transfers between devices: 5.97 us -> 0 us
    all_gather x4 -> x0, waiting for transfers between devices: 176 us -> none  [the longest x1 119 us: on_device(): stripe = lax.all_gather(grad_rot, 'col', axis=0, tiled=True)]
    pallas_call x0 -> x1, Pallas kernels: none -> 161 us  [on_grid(): pl.pallas_call(functools.partial(kernel, token_count), out_shape=(jax.Sha...]
    psum x1 -> x0, waiting for transfers between devices: 66.6 us -> none  [on_device(): head_rotation_grad = lax.psum(head_term, ('row', 'col'))]
    dot_general x6 -> x0, matrix products: 43 us -> none  [the longest x1 16.2 us: on_device(): lax.dot_general(rotated_w, stripe, (((1,), (1,)), ((), ())), preferred_el...]
    all_to_all x1 -> x0, waiting for transfers between devices: 26 us -> none  [on_device(): lax.all_to_all(pieces, 'col', split_axis=0, concat_axis=0, tiled=True)]
    all_to_all x1 -> x0, blocking collectives: 12.1 us -> none  [on_device(): lax.all_to_all(stripe, 'row', split_axis=0, concat_axis=1, tiled=True)]
    convert_element_type x2 -> x0, local copies, waits for them, and re-layouts: 8.14 us -> none  [the longest x1 4.21 us: on_device(): rotated_w = rotated_w.reshape(v_full.shape).astype(jnp.bfloat16)]
    reshape x3 -> x0, local copies, waits for them, and re-layouts: 8.13 us -> none  [the longest x1 4.15 us: on_device(): carried.reshape(-1, DH)]
  transfers between devices with their start and end apart: 6 -> 0, of which waited for: 6 -> 0; matrix products, arithmetic and copies ran while one was open for 9% -> 0% of each run, Pallas kernels for 0% -> 0%
where the time goes in v2:
time: 177 us; the launch traced here: 176 us
  Pallas kernels  161 us (91%)
  local copies, waits for them, and re-layouts  12.4 us (7%)
  other arithmetic  2.73 us (2%)
    pallas_call x1, Pallas kernels, on_grid(): pl.pallas_call(functools.partial(kernel, token_count), out_shape=(jax.Sha...  161 us
    unnamed x4, local copies, waits for them, and re-layouts  12.4 us

profile of v2, /device:TPU:0, one launch (start us, length us, event | category | flops | bytes accessed | tf_op | source)
XLA Modules:
  0.0 176.4 jit_solution(8031527597074970816)
XLA Ops:
  0.6 1.3 multiply_exponential_fusion
  1.9 1.5 convert_element_type.7.head_half
  3.4 160.6 %shard_map.86 = (f32[1024,4096]{1,0:T(8,128)}, f32[128,128]{1,0:T(8,128)}) custom-call(bf16[512,1024]{1,0:T(8,128)(2,1)} %hidden.1, bf16[128,512]{1,0:T(8,128)(2,1)} %target.1, bf16[1024,512]{1,0:T(8,128)(2,1)} %v_weight.1, s32[1024,512]{1,0:T(8,128)} %codes.1, f32[1,512]{1,0:T(1,128)} %bitcast.1, bf16[128,128]{1,0:T(8,128)(2,1)} %convert_element_type.7.head_half, ...), custom_call_target="tpu_custom_call" | custom-call | tf_op jit(solution)/shard_map/pallas_call | solution.py:466
  164.0 0.0 copy-start
  164.0 11.8 %copy.11 = f32[1024,4096]{1,0:T(8,128)} copy(f32[1024,4096]{1,0:T(8,128)} %get-tuple-element.4) | data formatting | bytes 33554432
  175.8 0.0 copy-done
  175.8 0.6 copy.12
Async XLA Ops:
  164.0 11.8 %copy-start = (f32[128,128]{1,0:T(8,128)S(1)}, f32[128,128]{1,0:T(8,128)}, u32[]{:S(2)}) copy-start(f32[128,128]{1,0:T(8,128)} %get-tuple-element.5) | copy-start | bytes 196612

commit v3 on v2

--- a/solution.py
+++ b/solution.py
@@ -81,8 +81,9 @@
     g_own,
     g_all,
     rot32,
-    rot16,
-    carried,
+    vt,
+    ut,
+    head_sum,
     stage,
     head_term,
     head_in,
@@ -145,14 +146,11 @@
     swap_h = copy(hidden, hid.at[r], swap_send.at[0], swap_recv.at[0], c, 1 - r)
     swap_v = copy(v_weight, vf.at[r], swap_send.at[1], swap_recv.at[1], c, 1 - r)
     swap_h.start()
-    swap_v.start()
-    hid[r] = hidden[...]
-    vf[r] = v_weight[...]
 
     quantized = (codes[...].astype(F32) * scales[...]).astype(BF16)
 
-    def partial_half(h):
-        product = jnp.dot(hid[h], quantized, preferred_element_type=F32)
+    def partial_half(h, tokens):
+        product = jnp.dot(tokens[...], quantized, preferred_element_type=F32)
         for i in range(ZS):
             owner = h * ZS + i
             rows = product[i * piece : (i + 1) * piece]
@@ -175,31 +173,39 @@
 
         lax.fori_loop(0, ZS, send, 0)
 
-    partial_half(r)
+    partial_half(r, hidden)
     swap_h.wait_recv()
-    partial_half(1 - r)
-
-    def round_rotation(b):
+    swap_v.start()
+    partial_half(1 - r, hid.at[1 - r])
+    hid[r] = hidden[...]
+    vf[r] = v_weight[...]
+
+    def fold_rotation(b):
         rot_copy(b).wait()
 
         def body(i, carry):
-            rows = pl.ds(pl.multiple_of(i * 128, 128), 128)
-            rot16[b, rows, :] = rot32[b % 2, rows, :].astype(BF16)
+            at = pl.ds(pl.multiple_of(i * wtile, wtile), wtile)
+            ut[b, :, at] = jnp.dot(
+                vt[...], rot32[b % 2, :, at].astype(BF16), preferred_element_type=F32
+            ).astype(BF16)
             return carry
 
-        lax.fori_loop(0, width // 128, body, 0)
+        lax.fori_loop(0, width // wtile, body, 0)
         if b + 2 < ZS:
             rot_copy(b + 2).start()
 
-    round_rotation(0)
-    round_rotation(1)
     swap_v.wait_recv()
+    for k in range(2):
+        vt[k * chans : (k + 1) * chans, :] = vf[k].T
+    fold_rotation(0)
+    fold_rotation(1)
     for k in range(2):
         for n in range(chans // DH):
             cut = slice(n * DH, (n + 1) * DH)
             rw[k, :, cut] = jnp.dot(
                 vf[k, :, cut], head_half[...], preferred_element_type=F32
             ).astype(BF16)
+    fold_rotation(2)
 
     total = part_own[...] - target[...].astype(F32)
     for d in range(1, cols):
@@ -241,7 +247,6 @@
     sent = lambda cp: cp.wait_send()
 
     ag_first(start)
-    round_rotation(2)
     for d in range(1, ZS):
 
         @pl.when(z >= d)
@@ -256,7 +261,7 @@
             ag_copy(s, ag_z.at[s], c).wait_recv()
             ag_next(s, False, start)
 
-    round_rotation(3)
+    fold_rotation(3)
     for zz in range(ZS):
         s = 2 * zz + 1 - x
         ag_copy(s, ag_z.at[s], c).wait_recv()
@@ -313,10 +318,27 @@
         def _():
             act(g_copy(block, slot, k, g_z.at[i], c - 2, r))
 
-        @pl.when(zs != z)
+        crosses = zs != z
+        if k == 1:
+            crosses = crosses & (zs != end)
+
+        @pl.when(crosses)
         def _():
             act(g_copy(block, slot, k, g_x.at[i], 2 * z + 1 - x, r))
 
+    def g_beside(act):
+        slot = lax.rem(2 * end + 1 - x, ZS)
+        i = slot * 2 + 1
+
+        @pl.when((r == 0) & (z < ZS - 1))
+        def _():
+            act(g_copy(g_all.at[slot, 1], slot, 1, g_z.at[i], c + 2, r))
+
+        @pl.when((r == 1) & (z > 0))
+        def _():
+            act(g_copy(g_all.at[slot, 1], slot, 1, g_z.at[i], c - 2, r))
+
+    end = (ZS - 1) * r
     near = jnp.clip(z, 2 * r, 2 * r + 1)
     far = 4 * r + 1 - near
 
@@ -325,7 +347,7 @@
             stage.at[n], rot_grad.at[:, pl.ds(pl.multiple_of(slot * width, 128), width)], out_sem.at[n]
         )
 
-    def work(slot, n, first):
+    def work(slot, n):
         if n >= 2:
             out_copy(slot, n % 2).wait()
 
@@ -342,50 +364,68 @@
         lax.fori_loop(0, width // wtile, outputs, 0)
         out_copy(slot, n % 2).start()
 
-        def carry_on(i, carry):
-            k = i // (chans // tile)
-            cut = pl.ds(pl.multiple_of(lax.rem(i, chans // tile) * tile, tile), tile)
-            product = jnp.dot(rot16[slot], g_all[slot, k, :, cut], preferred_element_type=F32)
-            if first:
-                carried[k, :, cut] = product
-            else:
-                carried[k, :, cut] += product
+        pairs = chans // (2 * DH)
+
+        def heads(i, carry):
+            k = i // pairs
+            rows = pl.ds(pl.multiple_of(i * 2 * DH, 2 * DH), 2 * DH)
+            cut = pl.ds(pl.multiple_of(lax.rem(i, pairs) * 2 * DH, 2 * DH), 2 * DH)
+            head_sum[...] += jnp.dot(
+                ut[slot, rows, :], g_all[slot, k, :, cut], preferred_element_type=F32
+            )
             return carry
 
-        lax.fori_loop(0, 2 * (chans // tile), carry_on, 0)
+        lax.fori_loop(0, 2 * pairs, heads, 0)
 
     def g_wait(slot, k):
         copy(g_own, g_all.at[slot, k], g_src.at[0], g_recv.at[slot * 2 + k], c, r).wait_recv()
 
-    n = 0
-    for zs in (near, far):
-        slot = lax.rem(2 * zs + x, ZS)
-        for k in range(2):
-
-            @pl.when((zs != z) | (r != k))
-            def _():
-                g_wait(slot, k)
-
-            g_next(zs, k, start)
-        work(slot, n, n == 0)
-        n += 1
-    for zs in (near, far):
-        slot = lax.rem(2 * zs + 1 - x, ZS)
-        for k in range(2):
-            g_wait(slot, k)
-        work(slot, n, False)
-        n += 1
-
-    term = jnp.zeros((DH, DH), F32)
+    near_own, far_own = lax.rem(2 * near + x, ZS), lax.rem(2 * far + x, ZS)
+    near_off, far_off = lax.rem(2 * near + 1 - x, ZS), lax.rem(2 * far + 1 - x, ZS)
+    early = z + (ZS - 1) * r == ZS - 1
+
+    head_sum[...] = jnp.zeros_like(head_sum)
     for k in range(2):
-        for n in range(chans // DH):
-            cut = slice(n * DH, (n + 1) * DH)
-            term = term + lax.dot_general(
-                vf[k, :, cut],
-                carried[k, :, cut].astype(BF16),
-                (((0,), (0,)), ((), ())),
-                preferred_element_type=F32,
-            )
+
+        @pl.when((near != z) | (r != k))
+        def _():
+            g_wait(near_own, k)
+
+        g_next(near, k, start)
+    work(near_own, 0)
+
+    @pl.when(early)
+    def _():
+        g_wait(near_off, 0)
+        g_wait(near_off, 1)
+        work(near_off, 1)
+
+    for k in range(2):
+        g_wait(far_own, k)
+        g_next(far, k, start)
+    g_wait(lax.rem(2 * end + 1 - x, ZS), 1)
+    g_beside(start)
+
+    @pl.when(jnp.logical_not(early))
+    def _():
+        g_wait(near_off, 0)
+
+        @pl.when(near != end)
+        def _():
+            g_wait(near_off, 1)
+
+        work(near_off, 1)
+
+    work(far_own, 2)
+    g_wait(far_off, 0)
+
+    @pl.when(far != end)
+    def _():
+        g_wait(far_off, 1)
+
+    work(far_off, 3)
+
+    term = head_sum[:DH, :DH] + head_sum[DH:, DH:]
     share = DH // people
     head_term[...] = term.reshape(people, share, DH)
 
@@ -449,6 +489,7 @@
     for zs in (near, far):
         for k in range(2):
             g_next(zs, k, sent)
+    g_beside(sent)
     out_copy(0, 0).wait()
     out_copy(0, 1).wait()
 
@@ -482,8 +523,9 @@
             pltpu.VMEM((width, chans), BF16),
             pltpu.VMEM((ZS, 2, width, chans), BF16),
             pltpu.VMEM((2, width, width), F32),
-            pltpu.VMEM((ZS, width, width), BF16),
-            pltpu.VMEM((2, width, chans), F32),
+            pltpu.VMEM((2 * chans, width), BF16),
+            pltpu.VMEM((ZS, 2 * chans, width), BF16),
+            pltpu.VMEM((2 * DH, 2 * DH), F32),
             pltpu.VMEM((2, width, width), F32),
             pltpu.VMEM((people, DH // people, DH), F32),
             pltpu.VMEM((people, DH // people, DH), F32),

time: 177 us -> 169 us (0.955)
  Pallas kernels: 161 us -> 153 us
    pallas_call x1, Pallas kernels: 161 us -> 153 us  [on_grid(): pl.pallas_call(functools.partial(kernel, token_count), out_shape=(jax.Sha...]
where the time goes in v3:
time: 169 us
  Pallas kernels  153 us (91%)
  local copies, waits for them, and re-layouts  12.4 us (7%)
  other arithmetic  2.73 us (2%)
    pallas_call x1, Pallas kernels, on_grid(): pl.pallas_call(functools.partial(kernel, token_count), out_shape=(jax.Sha...  153 us
    unnamed x4, local copies, waits for them, and re-layouts  12.4 us

profile of v3, /device:TPU:0, one launch (start us, length us, event | category | flops | bytes accessed | tf_op | source)
XLA Modules:
  0.0 168.9 jit_solution(2735256988515744617)
XLA Ops:
  0.6 1.3 multiply_exponential_fusion
  1.9 1.5 convert_element_type.7.head_half
  3.4 153.1 %shard_map.86 = (f32[1024,4096]{1,0:T(8,128)}, f32[128,128]{1,0:T(8,128)}) custom-call(bf16[512,1024]{1,0:T(8,128)(2,1)} %hidden.1, bf16[128,512]{1,0:T(8,128)(2,1)} %target.1, bf16[1024,512]{1,0:T(8,128)(2,1)} %v_weight.1, s32[1024,512]{1,0:T(8,128)} %codes.1, f32[1,512]{1,0:T(1,128)} %bitcast.1, bf16[128,128]{1,0:T(8,128)(2,1)} %convert_element_type.7.head_half, ...), custom_call_target="tpu_custom_call" | custom-call | tf_op jit(solution)/shard_map/pallas_call | solution.py:507
  156.5 0.0 copy-start
  156.5 11.8 %copy.11 = f32[1024,4096]{1,0:T(8,128)} copy(f32[1024,4096]{1,0:T(8,128)} %get-tuple-element.4) | data formatting | bytes 33554432
  168.3 0.0 copy-done
  168.3 0.6 copy.12
Async XLA Ops:
  156.5 11.8 %copy-start = (f32[128,128]{1,0:T(8,128)S(1)}, f32[128,128]{1,0:T(8,128)}, u32[]{:S(2)}) copy-start(f32[128,128]{1,0:T(8,128)} %get-tuple-element.5) | copy-start | bytes 196612

commit v4 on v3

--- a/solution.py
+++ b/solution.py
@@ -205,7 +205,6 @@
             rw[k, :, cut] = jnp.dot(
                 vf[k, :, cut], head_half[...], preferred_element_type=F32
             ).astype(BF16)
-    fold_rotation(2)
 
     total = part_own[...] - target[...].astype(F32)
     for d in range(1, cols):
@@ -247,6 +246,7 @@
     sent = lambda cp: cp.wait_send()
 
     ag_first(start)
+    fold_rotation(2)
     for d in range(1, ZS):
 
         @pl.when(z >= d)
@@ -347,7 +347,7 @@
             stage.at[n], rot_grad.at[:, pl.ds(pl.multiple_of(slot * width, 128), width)], out_sem.at[n]
         )
 
-    def work(slot, n):
+    def rotation_work(slot, n):
         if n >= 2:
             out_copy(slot, n % 2).wait()
 
@@ -364,6 +364,7 @@
         lax.fori_loop(0, width // wtile, outputs, 0)
         out_copy(slot, n % 2).start()
 
+    def head_work(slot):
         pairs = chans // (2 * DH)
 
         def heads(i, carry):
@@ -377,6 +378,10 @@
 
         lax.fori_loop(0, 2 * pairs, heads, 0)
 
+    def work(slot, n):
+        rotation_work(slot, n)
+        head_work(slot)
+
     def g_wait(slot, k):
         copy(g_own, g_all.at[slot, k], g_src.at[0], g_recv.at[slot * 2 + k], c, r).wait_recv()
 
@@ -423,7 +428,7 @@
     def _():
         g_wait(far_off, 1)
 
-    work(far_off, 3)
+    head_work(far_off)
 
     term = head_sum[:DH, :DH] + head_sum[DH:, DH:]
     share = DH // people
@@ -453,6 +458,7 @@
 
     for d in range(1, people):
         hs_copy(d).start()
+    rotation_work(far_off, 3)
     total = head_term[me]
     for d in range(1, people):
         s = lax.rem(me + d, people)

time: 169 us -> 166 us (0.982)
  Pallas kernels: 153 us -> 150 us
    pallas_call x1, Pallas kernels: 153 us -> 150 us  [on_grid(): pl.pallas_call(functools.partial(kernel, token_count), out_shape=(jax.Sha...]
where the time goes in v4:
time: 166 us; the launch traced here: 165 us
  Pallas kernels  150 us (90%)
  local copies, waits for them, and re-layouts  12.4 us (7%)
  other arithmetic  2.73 us (2%)
    pallas_call x1, Pallas kernels, on_grid(): pl.pallas_call(functools.partial(kernel, token_count), out_shape=(jax.Sha...  150 us
    unnamed x4, local copies, waits for them, and re-layouts  12.4 us

profile of v4, /device:TPU:0, one launch (start us, length us, event | category | flops | bytes accessed | tf_op | source)
XLA Modules:
  0.0 165.3 jit_solution(5518476697818788800)
XLA Ops:
  0.6 1.3 multiply_exponential_fusion
  1.9 1.5 convert_element_type.7.head_half
  3.4 149.5 %shard_map.86 = (f32[1024,4096]{1,0:T(8,128)}, f32[128,128]{1,0:T(8,128)}) custom-call(bf16[512,1024]{1,0:T(8,128)(2,1)} %hidden.1, bf16[128,512]{1,0:T(8,128)(2,1)} %target.1, bf16[1024,512]{1,0:T(8,128)(2,1)} %v_weight.1, s32[1024,512]{1,0:T(8,128)} %codes.1, f32[1,512]{1,0:T(1,128)} %bitcast.1, bf16[128,128]{1,0:T(8,128)(2,1)} %convert_element_type.7.head_half, ...), custom_call_target="tpu_custom_call" | custom-call | tf_op jit(solution)/shard_map/pallas_call | solution.py:513
  152.9 0.0 copy-start
  152.9 11.8 %copy.11 = f32[1024,4096]{1,0:T(8,128)} copy(f32[1024,4096]{1,0:T(8,128)} %get-tuple-element.4) | data formatting | bytes 33554432
  164.7 0.0 copy-done
  164.7 0.6 copy.12
Async XLA Ops:
  152.9 11.8 %copy-start = (f32[128,128]{1,0:T(8,128)S(1)}, f32[128,128]{1,0:T(8,128)}, u32[]{:S(2)}) copy-start(f32[128,128]{1,0:T(8,128)} %get-tuple-element.5) | copy-start | bytes 196612
